TPU v7x, 32 devices: a whole 2x2x4 slice. The times are simulated.
32 devices in a mesh: grp: 2 (over x), lon: 16 (over z, y, core).
Axes of the slice: x: 2, y: 2, z: 4, core: 2. Of those that a mesh axis runs over, the one named last changes fastest.
Arguments:
- control: float32 [32, 512, 512], P('grp', 'lon'), parts along dimension 0, may hold values from -6 to 6
- std_field: float32 [16, 512, 512], P(None, 'lon'), may hold values from 0.5 to 2
- kappa_lon: float32 [512, 512], P('lon'), may hold values from 0.18 to 0.245
- kappa_lat: float32 [512, 512], P('lon'), may hold values from 0.18 to 0.245
- sea_mask: int32 [512, 512], P('lon'), may hold values 0 or 1
- vertical: float32 [16, 16], replicated, may hold values from -1.5 to 1.5
- block_index: int32 [32, 16, 8], P(('grp', 'lon')), parts along dimension 0, may hold values from 0 to 2047, as said below
- weights: float32 [32, 16, 8, 128], P(('grp', 'lon')), parts along dimension 0, may hold values from -1 to 1
- obs_value: float32 [32, 16, 8], P(('grp', 'lon')), parts along dimension 0, may hold values from -6 to 6
- obs_rinv: float32 [32, 16, 8], P(('grp', 'lon')), parts along dimension 0, may hold values from 0.5 to 4
- obs_count: int32 [32, 16], P(('grp', 'lon')), parts along dimension 0, may hold values from 0 to 8, as said below
Outputs:
- gradient: float32 [32, 512, 512], P('grp', 'lon'), parts along dimension 0
- departure: float32 [32, 16, 8], P(('grp', 'lon')), parts along dimension 0
There are 2 independent parts, one for each index of `grp`. A program takes and returns all parts, laid end to end along the dimension named above; an argument that names none is the same for every part. Nothing has to cross between parts.
Inputs may be any that keep to these rules, and one draw needn't show every extreme that they name: Slot c of owner p for tile t holds an observation exactly when c < obs_count[p, t]; in every draw one tile has 8 observations from every owner. `block_index`: each slot names one stencil block of its tile.
All inputs are finite; a program needn't handle non-finite values. No bound on the sum of `sea_mask` on one device may be relied on, other than what follows from the above.
Results may differ from a plain program's by a relative error of at most 0.000067.
Values sent between devices are 32-bit elements; how exact they have to be, the bound alone decides.
No kernel may reach another device: no remote copies, remote signals or barrier semaphores. Data moves between devices by JAX's collectives and lax.ppermute only.
A program may use at most 64 MiB of HBM per device.

v0:
```python
import jax
import jax.numpy as jnp
from jax import lax
from jax.experimental import pallas as pl
from jax.experimental.pallas import tpu as pltpu
from jax.sharding import PartitionSpec as P

STEN = 128
PASSES = 10
WIDE = 256
F32 = jnp.float32
BF16 = jnp.bfloat16
WHOLE_VMEM = 60 * 1024 * 1024
TIERS = ((0, 4), (4, PASSES))
VMEM_LIMIT = 24 * 1024 * 1024

VMEM_SPEC = pl.BlockSpec(memory_space=pltpu.VMEM)
SMEM_SPEC = pl.BlockSpec(memory_space=pltpu.SMEM)


def split(x):
    high = x.astype(BF16)
    return high, (x - high.astype(F32)).astype(BF16)


def split3(x):
    high = x.astype(BF16)
    rest = x - high.astype(F32)
    middle = rest.astype(BF16)
    return high, middle, (rest - middle.astype(F32)).astype(BF16)


def dot(a, b):
    return jnp.dot(a, b, preferred_element_type=F32)


def log2(n):
    assert n & (n - 1) == 0
    return n.bit_length() - 1


def iota(shape, dim):
    return lax.broadcasted_iota(jnp.int32, shape, dim)


def onehot(condition):
    return jnp.where(condition, F32(1.0), F32(0.0)).astype(BF16)


def product(left, right):
    (lh, ll), (rh, rl) = left, right
    return dot(lh, rh) + (dot(lh, rl) + dot(ll, rh))


def mixing_matrix(vertical):
    levels = vertical.shape[0]
    group = WIDE // levels
    expand = onehot(iota((levels, WIDE), 1) // group == iota((levels, WIDE), 0))
    keep = iota((WIDE, WIDE), 0) // levels == iota((WIDE, WIDE), 1) % group
    out = []
    for part in split(vertical):
        rows = dot(part, expand)
        tiled = jnp.concatenate([rows] * group, axis=0)
        out.append(jnp.where(keep, tiled, F32(0.0)).astype(BF16))
    return tuple(out)


def mixing_matrix_back(vertical):
    levels = vertical.shape[0]
    group = WIDE // levels
    spread = onehot(iota((levels, WIDE), 1) % levels == iota((levels, WIDE), 0))
    repeat = onehot(iota((WIDE, levels), 0) // group == iota((WIDE, levels), 1))
    keep = iota((WIDE, WIDE), 0) % group == iota((WIDE, WIDE), 1) // levels
    out = []
    for part in split(vertical):
        rows = lax.dot_general(part, spread, (((0,), (0,)), ((), ())), preferred_element_type=F32)
        rows = rows.astype(BF16)
        out.append(jnp.where(keep, dot(repeat, rows), F32(0.0)).astype(BF16))
    return tuple(out)


def deinterleave(lat):
    parts = lat // STEN
    target = iota((lat, lat), 1)
    return onehot(iota((lat, lat), 0) == (target % STEN) * parts + target // STEN)


def interleave(lat):
    parts = lat // STEN
    source = iota((lat, lat), 0)
    return onehot(iota((lat, lat), 1) == (source % STEN) * parts + source // STEN)


def spread_block(lat):
    parts = lat // STEN
    target = iota((STEN, lat), 1)
    return onehot(iota((STEN, lat), 0) == (target % (STEN // parts)) * parts + target // STEN)


def lane_segment(rows, lat):
    parts = lat // STEN
    return (iota((rows, lat), 1) % STEN) // (STEN // parts)


def move(x, matrix):
    return tuple(dot(part, matrix).astype(BF16) for part in x)


def pack_meta(slots, values):
    stacked = jnp.concatenate(values, axis=0)
    eye = onehot(iota((stacked.shape[0], STEN), 0) == iota((stacked.shape[0], STEN), 1))
    return sum(
        lax.dot_general(part, eye, (((0,), (0,)), ((), ())), preferred_element_type=F32)
        for part in split3(stacked)
    )


def unpack_meta(recv_ref, slots, field):
    owners = recv_ref.shape[0]
    total = owners * slots
    rows = jnp.broadcast_to(recv_ref[:, slots : slots + 1, :], (owners, slots, STEN)).reshape(total, STEN)
    wanted = (iota((total, STEN), 0) & (slots - 1)) + field * slots
    return jnp.sum(jnp.where(iota((total, STEN), 1) == wanted, rows, F32(0.0)), axis=1, keepdims=True)


def head_kernel(
    mask_hbm, klon_hbm, klat_hbm, v_hbm, control_hbm, mixed_ref, faces_ref, left_ref, right_ref,
    mask_ref, klon_ref, klat_ref, v_ref, control_ref, sems,
):
    pairs = (
        (mask_hbm, mask_ref), (klon_hbm, klon_ref), (klat_hbm, klat_ref), (v_hbm, v_ref), (control_hbm, control_ref),
    )
    copies = [pltpu.make_async_copy(source, target, sems.at[k]) for k, (source, target) in enumerate(pairs)]
    for copy in copies:
        copy.start()
    levels, cols, lat = control_ref.shape
    parts = lat // STEN
    group = WIDE // levels
    halo = PASSES
    edge = halo * levels
    place = deinterleave(lat)
    for copy in copies[:4]:
        copy.wait()
    matrix = mixing_matrix(v_ref[...])
    wet = mask_ref[...].astype(F32)
    east = jnp.where(iota((cols, lat), 0) == cols - 1, F32(1.0), pltpu.roll(wet, cols - 1, 0))
    north = jnp.where(iota((cols, lat), 1) == lat - 1, F32(0.0), pltpu.roll(wet, lat - 1, 1))
    for k, face in enumerate((klon_ref[...] * wet * east, klat_ref[...] * wet * north, wet)):
        held = sum(dot(piece, place) for piece in (split3(face) if k < 2 else (face.astype(BF16),)))
        for q in range(parts):
            faces_ref[k * parts + q] = held[:, q * STEN : (q + 1) * STEN]
    copies[4].wait()
    for g in range(cols // group):
        x = control_ref[:, g * group : (g + 1) * group, :].reshape(WIDE, lat)
        y = product(matrix, move(split(x), place))
        for q in range(parts):
            mixed_ref[q, g * WIDE : (g + 1) * WIDE, :] = y[:, q * STEN : (q + 1) * STEN]
    for out, start in ((left_ref, 0), (right_ref, cols - halo)):
        for q in range(parts):
            out[q * edge : (q + 1) * edge, :] = mixed_ref[q, start * levels : start * levels + edge, :]
        for k in range(2 * parts):
            first = parts * edge + k * halo
            out[first : first + halo, :] = faces_ref[k, start : start + halo, :]
        first = parts * edge + 2 * parts * halo
        for q in range(parts):
            out[first + q : first + q + 1, :] = faces_ref[2 * parts + q, 0:1, :]
        out[first + parts :, :] = jnp.zeros((out.shape[0] - first - parts, STEN), F32)


def pack(index_ref, value_ref, rinv_ref, count_ref, weights_ref, sent_ref):
    owners, slots, _ = weights_ref.shape
    sent_ref[:, 0:slots, :] = weights_ref[...]
    valid = jnp.where(iota((slots, owners), 0) < count_ref[...], F32(1.0), F32(0.0))
    meta = pack_meta(slots, [value_ref[...], rinv_ref[...], index_ref[...].astype(F32), valid])
    sent_ref[:, slots:, :] = jnp.broadcast_to(meta[:, None, :], (owners, slots, STEN))


def hold_faces(ref, lon_ref, lat_ref, count):
    parts = lon_ref.shape[0]
    shape = (8, STEN)
    for c in range(count):
        rows = slice(8 * c, 8 * c + 8)
        for q in range(parts):
            lat_row = ref[parts + q, c : c + 1, :]
            lon_ref[q, rows, :] = jnp.broadcast_to(ref[q, c : c + 1, :], shape)
            lat_ref[q, rows, :] = jnp.broadcast_to(lat_row, shape)
            if q == parts - 1:
                lat_ref[parts, rows, :] = jnp.broadcast_to(pltpu.roll(lat_row, 1, 1), shape)


def join_faces(faces_ref, from_left, from_right, all_ref, levels):
    halo = PASSES
    cols = faces_ref.shape[1]
    parts = faces_ref.shape[0] // 3
    first = parts * halo * levels

    def far(source, k, c):
        at = first + k * halo + c
        return source[at : at + 1, :]

    for q in range(parts):
        at = first + 2 * parts * halo + q
        for k in (q, parts + q):
            all_ref[k, 0:halo, :] = from_left[first + k * halo : first + (k + 1) * halo, :]
            all_ref[k, halo : halo + cols, :] = faces_ref[k]
            all_ref[k, halo + cols : 2 * halo + cols, :] = from_right[first + k * halo : first + (k + 1) * halo, :]
        all_ref[q, halo - 1 : halo, :] = far(from_left, q, halo - 1) * faces_ref[2 * parts + q, 0:1, :]
        all_ref[q, halo + cols - 1 : halo + cols, :] = faces_ref[q, cols - 1 : cols, :] * from_right[at : at + 1, :]


def add_ghosts(ref, first, values):
    count = values[0].shape[0]
    parts = len(values)
    ref[parts, first : first + count, :] = pltpu.roll(values[0], STEN - 1, 1)
    ref[parts + 1, first : first + count, :] = pltpu.roll(values[-1], 1, 1)


def fill(ref, first, values):
    for q, value in enumerate(values):
        ref[q, first : first + value.shape[0], :] = value
    add_ghosts(ref, first, values)


def column_steps(src, dst, lon_ref, lat_ref, levels, low, high, step=0, face=0):
    parts = lon_ref.shape[0]
    halves = range(levels // 8)

    def load(k, c, h):
        return src[k, c * levels + 8 * h : c * levels + 8 * h + 8, :]

    def rate(ref, k, c):
        return ref[k, pl.ds(pl.multiple_of(8 * (c + face), 8), 8), :]

    here = [[load(q, low, h) for q in range(parts)] for h in halves]
    west = [[rate(lon_ref, q, low - 1) * (here[h][q] - load(q, low - 1, h)) for q in range(parts)] for h in halves]
    for c in range(low, high):
        lon = [rate(lon_ref, q, c) for q in range(parts)]
        lat = [rate(lat_ref, q, c) for q in range(parts + 1)]
        for h in halves:
            line = here[h]
            east = [load(q, c + 1, h) for q in range(parts)]
            flux_east = [lon[q] * (east[q] - line[q]) for q in range(parts)]
            ahead = line[1:] + [load(parts, c, h)]
            flux_north = [lat[parts] * (line[0] - load(parts + 1, c, h))]
            flux_north += [lat[q] * (ahead[q] - line[q]) for q in range(parts)]
            out = [
                line[q] + (flux_east[q] - west[h][q]) + (flux_north[q + 1] - flux_north[q])
                for q in range(parts)
            ]
            first = (c + step) * levels + 8 * h
            for q in range(parts):
                dst[q, first : first + 8, :] = out[q]
            add_ghosts(dst, first, out)
            here[h], west[h] = east, flux_east


def diffuse(a_ref, b_ref, lon_ref, lat_ref, levels, before_pass=None):
    width = a_ref.shape[1] // levels

    for first, last in TIERS:

        def pair(turn, carry):
            for k, (src, dst) in enumerate(((a_ref, b_ref), (b_ref, a_ref))):
                if before_pass is not None:
                    before_pass(2 * turn + k, src)
                column_steps(src, dst, lon_ref, lat_ref, levels, first + 1 + k, width - first - 1 - k)
            return carry

        lax.fori_loop(first // 2, last // 2, pair, 0)


def inner_kernel(
    mixed_ref, faces_ref, index_ref, value_ref, rinv_ref, count_ref, weights_ref,
    inner_ref, strips_ref, sent_ref, a_ref, b_ref, lon_ref, lat_ref,
):
    parts, own_rows, _ = mixed_ref.shape
    cols = faces_ref.shape[1]
    levels = own_rows // cols
    pack(index_ref, value_ref, rinv_ref, count_ref, weights_ref, sent_ref)
    hold_faces(faces_ref, lon_ref, lat_ref, cols)
    fill(a_ref, 0, [mixed_ref[q] for q in range(parts)])

    def save(turn, src):
        for side, (line, other) in enumerate(((turn, turn + 1), (cols - 1 - turn, cols - 2 - turn))):
            line = pl.ds(pl.multiple_of(line * levels, levels), levels)
            other = pl.ds(pl.multiple_of(other * levels, levels), levels)
            for q in range(parts):
                strips_ref[turn, side, q] = src[q, line, :]
                strips_ref[turn, side, parts + q] = src[q, other, :]

    diffuse(a_ref, b_ref, lon_ref, lat_ref, levels, save)
    for q in range(parts):
        inner_ref[q] = a_ref[q, PASSES * levels : (cols - PASSES) * levels, :]


def block_place(index, cols, parts):
    return (
        lax.shift_right_logical(index, log2(cols * parts)),
        lax.shift_right_logical(index, log2(parts)) & (cols - 1),
        index & (parts - 1),
    )


def weights_kernel(place_ref, recv_ref, std_ref, mask_ref, out_ref, held_ref, pick_ref, std_rows, wet_rows):
    owners, rows, _ = recv_ref.shape
    slots = rows // 2
    total = owners * slots
    levels, cols, lat = std_ref.shape
    parts = lat // STEN
    for s in range(parts):
        part = slice(s * STEN, (s + 1) * STEN)
        wet_rows[s * cols : (s + 1) * cols, :] = mask_ref[:, part].astype(F32)
        for a in range(levels):
            first = (a * parts + s) * cols
            std_rows[first : first + cols, :] = std_ref[a, :, part]

    def pick(o, carry):
        for k in range(slots):
            slot = o * slots + k
            level, column, seg = block_place(place_ref[0, slot], cols, parts)
            value = std_rows[pl.ds((level * parts + seg) * cols + column, 1), :]
            wet = wet_rows[pl.ds(seg * cols + column, 1), :]
            pick_ref[pl.ds(slot, 1), :] = value * wet
        return carry

    lax.fori_loop(0, owners, pick, 0)
    ws = recv_ref[:, 0:slots, :].reshape(total, STEN) * pick_ref[...]
    out_ref[...] = ws
    place = spread_block(lat)
    segs = unpack_meta(recv_ref, slots, 2).astype(jnp.int32) & (parts - 1)
    for j in range(total // STEN):
        part = slice(j * STEN, (j + 1) * STEN)
        seg = segs[part]
        held = sum(dot(piece, place) for piece in split3(ws[part]))
        held = jnp.where(lane_segment(STEN, lat) == seg, held, F32(0.0))
        for q in range(parts):
            held_ref[q, part, :] = held[:, q * STEN : (q + 1) * STEN]


def to_row(column):
    eye = iota((STEN, STEN), 0) == iota((STEN, STEN), 1)
    return jnp.sum(jnp.where(eye, column, F32(0.0)), axis=0, keepdims=True)


def to_column(row):
    eye = iota((STEN, STEN), 0) == iota((STEN, STEN), 1)
    return jnp.sum(jnp.where(eye, row, F32(0.0)), axis=1, keepdims=True)


def edge_kernel(
    inner_ref, strips_ref, from_left, from_right, faces_ref,
    rows_ref, all_ref, left_a, left_b, right_a, right_b, lon_ref, lat_ref,
):
    halo = PASSES
    levels = strips_ref.shape[3]
    parts = inner_ref.shape[0]
    cols = faces_ref.shape[1]
    edge = halo * levels
    join_faces(faces_ref, from_left, from_right, all_ref, levels)
    hold_faces(all_ref, lon_ref, lat_ref, cols + 2 * halo)
    fill(left_a, 0, [from_left[q * edge : (q + 1) * edge, :] for q in range(parts)])
    fill(right_a, 2 * levels, [from_right[q * edge : (q + 1) * edge, :] for q in range(parts)])

    def pair(turn, carry):
        for k, (left, left_to, right, right_to) in enumerate(
            ((left_a, left_b, right_a, right_b), (left_b, left_a, right_b, right_a))
        ):
            now = 2 * turn + k
            for side, ref, line, other in ((0, left, halo, halo + 1), (1, right, 1, 0)):
                fill(ref, line * levels, [strips_ref[now, side, q] for q in range(parts)])
                for q in range(parts):
                    ref[q, other * levels : (other + 1) * levels, :] = strips_ref[now, side, parts + q]
            column_steps(left, left_to, lon_ref, lat_ref, levels, 1, halo + 1, -1, now)
            column_steps(right, right_to, lon_ref, lat_ref, levels, 1, halo + 1, 1, halo + cols - 2 - now)
        return carry

    lax.fori_loop(0, PASSES // 2, pair, 0)
    for q in range(parts):
        rows_ref[q, 0:edge, :] = left_a[q, 0:edge, :]
        rows_ref[q, edge : cols * levels - edge, :] = inner_ref[q]
        rows_ref[q, cols * levels - edge :, :] = right_a[q, 2 * levels : 2 * levels + edge, :]


def departure_kernel(place_ref, rows_ref, recv_ref, ws_ref, held_ref, spread_ref, departure_ref, pick_ref):
    parts = rows_ref.shape[0]
    owners, rows, _ = recv_ref.shape
    slots = rows // 2
    total = owners * slots

    def pick(o, carry):
        for k in range(slots):
            slot = o * slots + k
            row = place_ref[1, slot]
            for q in range(parts):
                pick_ref[q, pl.ds(slot, 1), :] = rows_ref[q, pl.ds(row, 1), :]
        return carry

    lax.fori_loop(0, owners, pick, 0)
    value, rinv, index, valid = (unpack_meta(recv_ref, slots, field) for field in range(4))
    evolved = sum(pick_ref[q] * held_ref[q] for q in range(parts))
    evolved = jnp.sum(evolved, axis=1, keepdims=True)
    departure = jnp.where(valid > 0.5, evolved - value, F32(0.0))
    scaled = rinv * departure
    spread_ref[0:total, :] = scaled * ws_ref[...]
    spread_ref[total:, :] = jnp.zeros((spread_ref.shape[0] - total, STEN), F32)
    for j in range(total // STEN):
        part = slice(j * STEN, (j + 1) * STEN)
        spread_ref[total + j : total + j + 1, :] = to_row(index[part])
    lanes = jnp.where(iota((total, STEN), 1) == (iota((total, STEN), 0) & (slots - 1)), departure, F32(0.0))
    departure_ref[...] = jnp.sum(lanes.reshape(owners, slots, STEN), axis=1)


def second_kernel(
    v_ref, control_ref, own_ref, left_ref, right_ref, all_ref,
    out_ref, a_ref, b_ref, lon_ref, lat_ref,
):
    halo = PASSES
    levels, cols, lat = control_ref.shape
    parts = lat // STEN
    edge = halo * levels
    total = own_ref.shape[0] // STEN * STEN
    hold_faces(all_ref, lon_ref, lat_ref, cols + 2 * halo)
    place = spread_block(lat)

    def scatter(source, first, count, step, target):
        pieces = []
        keys = []
        for j in range(total // STEN):
            index = source[total + j : total + j + 1, :].astype(jnp.int32)
            level, column, seg = block_place(index, cols, parts)
            keys.append((column - first) * levels + level)
            keep = lane_segment(STEN, lat) == to_column(seg.astype(F32)).astype(jnp.int32)
            held = [dot(piece, place) for piece in split(source[j * STEN : (j + 1) * STEN, :])]
            held = [jnp.where(keep, piece, F32(0.0)).astype(BF16) for piece in held]
            pieces.append(jnp.concatenate(held, axis=1))
        for c in range(0, count, step):
            rows = step * levels
            sums = jnp.zeros((rows, 2 * lat), F32)
            for key, piece in zip(keys, pieces):
                sums = sums + dot(onehot(iota((rows, STEN), 0) + c * levels == key), piece)
            sums = sums[:, :lat] + sums[:, lat:]
            fill(a_ref, (target + c) * levels, [sums[:, q * STEN : (q + 1) * STEN] for q in range(parts)])

    scatter(own_ref, 0, cols, 8, halo)
    scatter(left_ref, cols - halo, halo, halo // 2, 0)
    scatter(right_ref, 0, halo, halo // 2, halo + cols)
    diffuse(a_ref, b_ref, lon_ref, lat_ref, levels)
    matrix = mixing_matrix_back(v_ref[...])
    back = interleave(lat)
    group = WIDE // levels
    for g in range(cols // group):
        part = slice(g * group, (g + 1) * group)
        rows = slice(edge + g * WIDE, edge + (g + 1) * WIDE)
        x = jnp.concatenate([a_ref[q, rows, :] for q in range(parts)], axis=1)
        y = product(matrix, move(split(x), back)).reshape(levels, group, lat)
        out_ref[:, part, :] = control_ref[:, part, :] + y


def call(kernel, out_shape, specs, scratch, flops, moved, limit=VMEM_LIMIT):
    return pl.pallas_call(
        kernel,
        out_shape=out_shape,
        in_specs=specs,
        out_specs=jax.tree.map(lambda _: VMEM_SPEC, out_shape),
        scratch_shapes=list(scratch),
        cost_estimate=pl.CostEstimate(flops=flops, bytes_accessed=moved, transcendentals=0),
        compiler_params=pltpu.CompilerParams(vmem_limit_bytes=limit),
    )


def shape(*dims):
    return jax.ShapeDtypeStruct(dims, F32)


def local(
    control, std_field, kappa_lon, kappa_lat, sea_mask, vertical,
    block_index, weights, obs_value, obs_rinv, obs_count,
):
    levels, cols, lat = control.shape
    parts = lat // STEN
    owners, slots = block_index.shape[1:]
    total = owners * slots
    halo = PASSES
    width = cols + 2 * halo
    cells = width * levels * lat
    count = lax.axis_size("lon")
    to_right = [(i, (i + 1) % count) for i in range(count)]
    to_left = [((i + 1) % count, i) for i in range(count)]

    message = parts * halo * (levels + 2) + parts
    message = -(-message // 8) * 8
    plane = pltpu.VMEM((cols, lat), F32)
    hbm = pl.BlockSpec(memory_space=pltpu.HBM)
    mixed, faces, edge_left, edge_right = call(
        head_kernel,
        (
            shape(parts, cols * levels, STEN), shape(3 * parts, cols, STEN),
            shape(message, STEN), shape(message, STEN),
        ),
        [hbm] * 5,
        [
            pltpu.VMEM((cols, lat), jnp.int32), plane, plane, pltpu.VMEM((levels, levels), F32),
            pltpu.VMEM((levels, cols, lat), F32), pltpu.SemaphoreType.DMA((5,)),
        ],
        12 * cells * lat, 8 * 4 * cells, WHOLE_VMEM,
    )(sea_mask, kappa_lon, kappa_lat, vertical, control)
    from_left = lax.ppermute(edge_right, "lon", to_right)
    from_right = lax.ppermute(edge_left, "lon", to_left)

    inside = pltpu.VMEM((parts + 2, cols * levels, STEN), F32)
    wedge = pltpu.VMEM((parts + 2, (halo + 2) * levels, STEN), F32)
    inner, strips, sent = call(
        inner_kernel,
        (
            shape(parts, (cols - 2 * halo) * levels, STEN), shape(PASSES, 2, 2 * parts, levels, STEN),
            shape(owners, 2 * slots, STEN),
        ),
        [VMEM_SPEC] * 7,
        [
            inside, inside,
            pltpu.VMEM((parts, cols * 8, STEN), F32), pltpu.VMEM((parts + 1, cols * 8, STEN), F32),
        ],
        5 * PASSES * cells, PASSES * 4 * cells,
    )(
        mixed, faces, block_index[0].T, obs_value[0].T, obs_rinv[0].T, obs_count, weights[0]
    )
    recv = lax.all_to_all(sent, "lon", split_axis=0, concat_axis=0, tiled=True)
    field = pltpu.VMEM((parts + 2, width * levels, STEN), F32)
    faces_held = [pltpu.VMEM((parts, width * 8, STEN), F32), pltpu.VMEM((parts + 1, width * 8, STEN), F32)]
    rows, all_faces = call(
        edge_kernel,
        (shape(parts, cols * levels, STEN), shape(2 * parts, -(-width // 8) * 8, STEN)),
        [VMEM_SPEC] * 5,
        [wedge, wedge, wedge, wedge, *faces_held],
        5 * PASSES * cells, PASSES * 4 * cells,
    )(inner, strips, from_left, from_right, faces)
    recv, rows = lax.optimization_barrier((recv, rows))
    index = recv[:, slots, 2 * slots : 3 * slots].reshape(total).astype(jnp.int32)
    level, column, _ = block_place(index, cols, parts)
    places = jnp.stack([index, column * levels + level])
    ws, held = call(
        weights_kernel,
        (shape(total, STEN), shape(parts, total, STEN)),
        [SMEM_SPEC] + [VMEM_SPEC] * 3,
        [
            pltpu.VMEM((total, STEN), F32), pltpu.VMEM((levels * cols * parts, STEN), F32),
            pltpu.VMEM((cols * parts, STEN), F32),
        ],
        6 * total * STEN * lat, 4 * 4 * cells,
    )(places, recv, std_field, sea_mask)

    extra = -(-total // (8 * STEN)) * 8
    spread, departure = call(
        departure_kernel,
        (shape(total + extra, STEN), shape(owners, STEN)),
        [SMEM_SPEC] + [VMEM_SPEC] * 4,
        [pltpu.VMEM((parts, total, STEN), F32)],
        8 * total * lat, 4 * 4 * total * lat,
    )(places, rows, recv, ws, held)

    spread_left = lax.ppermute(spread, "lon", to_right)
    spread_right = lax.ppermute(spread, "lon", to_left)
    mine = lax.all_to_all(departure[:, None, :], "lon", split_axis=0, concat_axis=0, tiled=True)

    gradient = call(
        second_kernel, shape(levels, cols, lat), [VMEM_SPEC] * 6, [field, field, *faces_held],
        10 * PASSES * cells, 2 * PASSES * 4 * cells,
    )(vertical, control, spread, spread_left, spread_right, all_faces)
    gradient, mine = lax.optimization_barrier((gradient, mine))
    return gradient, mine[:, 0, :slots][None]


def solution(mesh):
    in_specs = (
        P("grp", "lon", None),
        P(None, "lon", None),
        P("lon", None),
        P("lon", None),
        P("lon", None),
        P(),
        P(("grp", "lon"), None, None),
        P(("grp", "lon"), None, None, None),
        P(("grp", "lon"), None, None),
        P(("grp", "lon"), None, None),
        P(("grp", "lon"), None),
    )
    out_specs = (P("grp", "lon", None), P(("grp", "lon"), None, None))
    return jax.shard_map(local, mesh=mesh, in_specs=in_specs, out_specs=out_specs, check_vma=False)
```

profile of v0, /device:TPU:0, one launch (start us, length us, event | category | flops | bytes accessed | tf_op | source)
XLA Modules:
  0.0 53.4 jit_solution(3880781618245733804)
XLA Ops:
  0.7 4.1 %shard_map.122 = (f32[4,512,128]{2,1,0:T(8,128)}, f32[12,32,128]{2,1,0:T(8,128)}, f32[728,128]{1,0:T(8,128)}, f32[728,128]{1,0:T(8,128)}) custom-call(s32[32,512]{1,0:T(8,128)} %mask_ref.1, f32[32,512]{1,0:T(8,128)} %klon_hbm.1, f32[32,512]{1,0:T(8,128)} %klat_hbm.1, f32[16,16]{1,0:T(8,128)} %v_ref.1, f32[16,32,512]{2,1,0:T(8,128)} %control_ref.1), custom_call_target="tpu_custom_call" | custom-call | flops 2617245696 | bytes 13631488 | tf_op jit(solution)/shard_map/pallas_call | solution.py:494
  4.8 0.5 collective-permute-start
  5.3 5.1 %collective-permute-start.1 = (f32[728,128]{1,0:T(8,128)}, f32[728,128]{1,0:T(8,128)S(1)}, u32[]{:S(2)}, u32[]{:S(2)}) collective-permute-start(f32[728,128]{1,0:T(8,128)} %get-tuple-element.25), channel_id=1, source_target_pairs={{1,0},{2,1},{3,2},{4,3},{5,4},{6,5},{7,6},{8,7},{9,8},{10,9},{11,1... | collective-permute-start | bytes 1118216 | tf_op jit(solution)/shard_map/ppermute | solution.py:508
  10.4 0.0 copy-start.1
  10.4 1.2 %copy-done.1 = f32[4,512,128]{2,1,0:T(8,128)S(1)} copy-done((f32[4,512,128]{2,1,0:T(8,128)S(1)}, f32[4,512,128]{2,1,0:T(8,128)}, u32[]{:S(2)}) %copy-start.1) | copy-done | bytes 1048600
  11.6 0.9 %copy-done.3 = f32[12,32,128]{2,1,0:T(8,128)S(1)} copy-done((f32[12,32,128]{2,1,0:T(8,128)S(1)}, f32[12,32,128]{2,1,0:T(8,128)}, u32[]{:S(2)}) %copy-start.3) | copy-done | bytes 196632
  12.5 3.2 %shard_map.123 = (f32[4,192,128]{2,1,0:T(8,128)S(1)}, f32[10,2,8,16,128]{4,3,2,1,0:T(8,128)S(1)}, f32[16,16,128]{2,1,0:T(8,128)}) custom-call(f32[4,512,128]{2,1,0:T(8,128)S(1)} %copy-done.1, f32[12,32,128]{2,1,0:T(8,128)S(1)} %copy-done.3, s32[8,16]{1,0:T(8,128)S(1)} %bitcast.16, f32[8,16]{1,0:T(8,128)S(1)} %bitcast.17, f32[8,16]{1,0:T(8,128)S(1)} %bitcast.18, ...), custom_call_target="tpu_custom_call" | custom-call | flops 21299200 | bytes 17039360 | tf_op jit(solution)/shard_map/pallas_call | solution.py:512
  15.7 0.7 %copy-done.5 = f32[4,192,128]{2,1,0:T(8,128)} copy-done((f32[4,192,128]{2,1,0:T(8,128)}, f32[4,192,128]{2,1,0:T(8,128)S(1)}, u32[]{:S(2)}) %copy-start.5) | copy-done | bytes 393240
  16.5 3.6 %all-to-all-start = ((f32[16,16,128]{2,1,0:T(8,128)}), f32[16,16,128]{2,1,0:T(8,128)S(1)}, u32[]{:S(2)}, u32[]{:S(2)}) async-start(f32[16,16,128]{2,1,0:T(8,128)} %get-tuple-element.21), calls=%async_computation | async-start | bytes 262144 | tf_op jit(solution)/shard_map/all_to_all | solution.py:527
  20.1 0.8 %copy-done.7 = f32[728,128]{1,0:T(8,128)} copy-done((f32[728,128]{1,0:T(8,128)}, f32[728,128]{1,0:T(8,128)S(1)}, u32[]{:S(2)}) %copy-start.7) | copy-done | bytes 372760
  20.9 0.7 %copy-done.9 = f32[728,128]{1,0:T(8,128)} copy-done((f32[728,128]{1,0:T(8,128)}, f32[728,128]{1,0:T(8,128)S(1)}, u32[]{:S(2)}) %copy-start.9) | copy-done | bytes 372760
  21.6 0.9 %copy-done.4 = f32[12,32,128]{2,1,0:T(8,128)S(1)} copy-done((f32[12,32,128]{2,1,0:T(8,128)S(1)}, f32[12,32,128]{2,1,0:T(8,128)}, u32[]{:S(2)}) %copy-start.4) | copy-done | bytes 196632
  22.5 1.0 %copy-done.6 = f32[4,192,128]{2,1,0:T(8,128)S(1)} copy-done((f32[4,192,128]{2,1,0:T(8,128)S(1)}, f32[4,192,128]{2,1,0:T(8,128)}, u32[]{:S(2)}) %copy-start.6) | copy-done | bytes 393240
  23.5 1.0 %copy-done.8 = f32[728,128]{1,0:T(8,128)S(1)} copy-done((f32[728,128]{1,0:T(8,128)S(1)}, f32[728,128]{1,0:T(8,128)}, u32[]{:S(2)}) %copy-start.8) | copy-done | bytes 372760
  24.5 1.0 %copy-done.10 = f32[728,128]{1,0:T(8,128)S(1)} copy-done((f32[728,128]{1,0:T(8,128)S(1)}, f32[728,128]{1,0:T(8,128)}, u32[]{:S(2)}) %copy-start.10) | copy-done | bytes 372760
  25.5 3.1 %shard_map.124 = (f32[4,512,128]{2,1,0:T(8,128)S(1)}, f32[8,56,128]{2,1,0:T(8,128)S(1)}) custom-call(f32[4,192,128]{2,1,0:T(8,128)S(1)} %copy-done.6, f32[10,2,8,16,128]{4,3,2,1,0:T(8,128)S(1)} %get-tuple-element.23.strips_ref, f32[728,128]{1,0:T(8,128)S(1)} %copy-done.8, f32[728,128]{1,0:T(8,128)S(1)} %copy-done.10, f32[12,32,128]{2,1,0:T(8,128)S(1)} %copy-done.4), custom_call_target="tpu_custom_call" | custom-call | flops 21299200 | bytes 17039360 | tf_op jit(solution)/shard_map/pallas_call | solution.py:530
  28.7 0.0 copy-start.11
  28.7 0.7 %copy-done.11 = f32[8,56,128]{2,1,0:T(8,128)} copy-done((f32[8,56,128]{2,1,0:T(8,128)}, f32[8,56,128]{2,1,0:T(8,128)S(1)}, u32[]{:S(2)}) %copy-start.11) | copy-done | bytes 229400
  29.3 0.0 all-to-all-done.recv_ref
  29.3 0.1 convert_reduce_fusion
  29.5 0.1 convert_element_type.18
  29.6 0.0 copy-start.14
  29.6 0.8 %copy-done.14 = s32[32,512]{1,0:T(8,128)S(1)} copy-done((s32[32,512]{1,0:T(8,128)S(1)}, s32[32,512]{1,0:T(8,128)}, u32[]{:S(2)}) %copy-start.14) | copy-done | bytes 65560
  30.4 1.4 %shard_map.125 = (f32[128,128]{1,0:T(8,128)S(1)}, f32[4,128,128]{2,1,0:T(8,128)S(1)}) custom-call(s32[2,128]{1,0:T(2,128)S(1)} %pad_add_fusion.place_ref, f32[16,16,128]{2,1,0:T(8,128)S(1)} %all-to-all-done.recv_ref, f32[16,32,512]{2,1,0:T(8,128)S(1)} %copy-done.2, s32[32,512]{1,0:T(8,128)S(1)} %copy-done.14), custom_call_target="tpu_custom_call" | custom-call | flops 50331648 | bytes 6815744 | tf_op jit(solution)/shard_map/pallas_call | solution.py:541
  31.9 0.0 copy-start.12
  31.9 1.7 %shard_map.126 = (f32[136,128]{1,0:T(8,128)S(1)}, f32[16,128]{1,0:T(8,128)}) custom-call(s32[2,128]{1,0:T(2,128)S(1)} %pad_add_fusion.place_ref, f32[4,512,128]{2,1,0:T(8,128)S(1)} %get-tuple-element.28.rows_ref, f32[16,16,128]{2,1,0:T(8,128)S(1)} %all-to-all-done.recv_ref, f32[128,128]{1,0:T(8,128)S(1)} %get-tuple-element.29.ws_ref, ...), custom_call_target="tpu_custom_call" | custom-call | flops 524288 | bytes 1048576 | tf_op jit(solution)/shard_map/pallas_call | solution.py:553
  33.6 4.4 %collective-permute-start.3 = (f32[136,128]{1,0:T(8,128)S(1)}, f32[136,128]{1,0:T(8,128)S(1)}, u32[]{:S(2)}, u32[]{:S(2)}) collective-permute-start(f32[136,128]{1,0:T(8,128)S(1)} %get-tuple-element.31.own_ref), channel_id=1, source_target_pairs={{1,0},{2,1},{3,2},{4,3},{5,4},{6,5},{7,6},{8,7},{9,8},{10,9},{11,1... | collective-permute-start | bytes 208904 | tf_op jit(solution)/shard_map/ppermute | solution.py:562
  37.9 5.8 %all-to-all-start.1 = ((f32[16,1,128]{2,1,0:T(1,128)}), f32[16,1,128]{2,1,0:T(1,128)S(1)}, u32[]{:S(2)}, u32[]{:S(2)}) async-start(f32[16,1,128]{2,1,0:T(1,128)} %bitcast.8), calls=%async_computation.1 | async-start | bytes 16384 | tf_op jit(solution)/shard_map/all_to_all | solution.py:563
  43.8 0.6 %collective-permute-done.2.left_ref = f32[136,128]{1,0:T(8,128)S(1)} collective-permute-done((f32[136,128]{1,0:T(8,128)S(1)}, f32[136,128]{1,0:T(8,128)S(1)}, u32[]{:S(2)}, u32[]{:S(2)}) %collective-permute-start.2) | collective-permute-done | bytes 69664 | tf_op jit(solution)/shard_map/ppermute | solution.py:561
  44.4 8.3 %shard_map.127 = f32[16,32,512]{2,1,0:T(8,128)} custom-call(f32[16,16]{1,0:T(8,128)S(1)} %copy-done.15, f32[16,32,512]{2,1,0:T(8,128)S(1)} %copy-done, f32[136,128]{1,0:T(8,128)S(1)} %get-tuple-element.31.own_ref, f32[136,128]{1,0:T(8,128)S(1)} %collective-permute-done.2.left_ref, f32[136,128]{1,0:T(8,128)S(1)} %collective-permute-done.3.right_ref, ...), custom_call_target="tpu_custom_call" | custom-call | flops 42598400 | bytes 34078720 | tf_op jit(solution)/shard_map/pallas_call | solution.py:565
  52.7 0.1 copy.16
  52.8 0.6 %slice_bitcast_fusion = f32[1,16,8]{1,2,0:T(8,128)} fusion(f32[16,1,128]{0,2,1:T(8,128)S(1)} %copy.16), kind=kLoop, calls=%fused_computation.1 | loop fusion | bytes 1024 | tf_op jit(solution)/shard_map/broadcast_in_dim;squeeze | solution.py:570
  (32 shorter events, 0.1 us)
Async XLA Ops:
  0.6 9.7 %copy-start.19 = (s32[1,16]{1,0:T(1,128)S(1)}, s32[1,16]{1,0:T(1,128)}, u32[]{:S(2)}) copy-start(s32[1,16]{1,0:T(1,128)} %count_ref.1) | copy-start | bytes 196
  0.6 9.7 %copy-start.18 = (f32[1,16,8]{1,2,0:T(8,128)S(1)}, f32[1,16,8]{1,2,0:T(8,128)}, u32[]{:S(2)}) copy-start(f32[1,16,8]{1,2,0:T(8,128)} %param.20) | copy-start | bytes 1540
  0.7 9.7 %copy-start.17 = (f32[1,16,8]{1,2,0:T(8,128)S(1)}, f32[1,16,8]{1,2,0:T(8,128)}, u32[]{:S(2)}) copy-start(f32[1,16,8]{1,2,0:T(8,128)} %param.19) | copy-start | bytes 1540
  0.7 9.7 %copy-start.13 = (f32[1,16,8,128]{3,2,1,0:T(8,128)S(1)}, f32[1,16,8,128]{3,2,1,0:T(8,128)}, u32[]{:S(2)}) copy-start(f32[1,16,8,128]{3,2,1,0:T(8,128)} %param.18) | copy-start | bytes 196612
  0.7 9.7 %copy-start.16 = (s32[1,16,8]{1,2,0:T(8,128)S(1)}, s32[1,16,8]{1,2,0:T(8,128)}, u32[]{:S(2)}) copy-start(s32[1,16,8]{1,2,0:T(8,128)} %param.17) | copy-start | bytes 1540
  4.8 15.3 %collective-permute-start = (f32[728,128]{1,0:T(8,128)}, f32[728,128]{1,0:T(8,128)S(1)}, u32[]{:S(2)}, u32[]{:S(2)}) collective-permute-start(f32[728,128]{1,0:T(8,128)} %get-tuple-element.24), channel_id=1, source_target_pairs={{0,1},{1,2},{2,3},{3,4},{4,5},{5,6},{6,7},{7,8},{8,9},{9,10},{10,1... | collective-permute-start | bytes 1118216 | tf_op jit(solution)/shard_map/ppermute | solution.py:507
  5.3 15.6 %collective-permute-start.1 = (f32[728,128]{1,0:T(8,128)}, f32[728,128]{1,0:T(8,128)S(1)}, u32[]{:S(2)}, u32[]{:S(2)}) collective-permute-start(f32[728,128]{1,0:T(8,128)} %get-tuple-element.25), channel_id=1, source_target_pairs={{1,0},{2,1},{3,2},{4,3},{5,4},{6,5},{7,6},{8,7},{9,8},{10,9},{11,1... | collective-permute-start | bytes 1118216 | tf_op jit(solution)/shard_map/ppermute | solution.py:508
  10.4 1.2 %copy-start.1 = (f32[4,512,128]{2,1,0:T(8,128)S(1)}, f32[4,512,128]{2,1,0:T(8,128)}, u32[]{:S(2)}) copy-start(f32[4,512,128]{2,1,0:T(8,128)} %get-tuple-element.19.mixed_ref) | copy-start | bytes 3145732
  11.6 0.9 %copy-start.3 = (f32[12,32,128]{2,1,0:T(8,128)S(1)}, f32[12,32,128]{2,1,0:T(8,128)}, u32[]{:S(2)}) copy-start(f32[12,32,128]{2,1,0:T(8,128)} %get-tuple-element.20.faces_ref) | copy-start | bytes 589828
  15.7 0.7 %copy-start.5 = (f32[4,192,128]{2,1,0:T(8,128)}, f32[4,192,128]{2,1,0:T(8,128)S(1)}, u32[]{:S(2)}) copy-start(f32[4,192,128]{2,1,0:T(8,128)S(1)} %get-tuple-element.22.inner_ref) | copy-start | bytes 1179652
  16.5 12.9 %all-to-all-start = ((f32[16,16,128]{2,1,0:T(8,128)}), f32[16,16,128]{2,1,0:T(8,128)S(1)}, u32[]{:S(2)}, u32[]{:S(2)}) async-start(f32[16,16,128]{2,1,0:T(8,128)} %get-tuple-element.21), calls=%async_computation | async-start | bytes 262144 | tf_op jit(solution)/shard_map/all_to_all | solution.py:527
  20.1 0.8 %copy-start.7 = (f32[728,128]{1,0:T(8,128)}, f32[728,128]{1,0:T(8,128)S(1)}, u32[]{:S(2)}) copy-start(f32[728,128]{1,0:T(8,128)S(1)} %collective-permute-done.from_left) | copy-start | bytes 1118212
  20.9 0.7 %copy-start.9 = (f32[728,128]{1,0:T(8,128)}, f32[728,128]{1,0:T(8,128)S(1)}, u32[]{:S(2)}) copy-start(f32[728,128]{1,0:T(8,128)S(1)} %collective-permute-done.1.from_right) | copy-start | bytes 1118212
  21.6 0.9 %copy-start.4 = (f32[12,32,128]{2,1,0:T(8,128)S(1)}, f32[12,32,128]{2,1,0:T(8,128)}, u32[]{:S(2)}) copy-start(f32[12,32,128]{2,1,0:T(8,128)} %get-tuple-element.20.faces_ref) | copy-start | bytes 589828
  22.5 1.0 %copy-start.6 = (f32[4,192,128]{2,1,0:T(8,128)S(1)}, f32[4,192,128]{2,1,0:T(8,128)}, u32[]{:S(2)}) copy-start(f32[4,192,128]{2,1,0:T(8,128)} %copy-done.5) | copy-start | bytes 1179652
  23.5 1.0 %copy-start.8 = (f32[728,128]{1,0:T(8,128)S(1)}, f32[728,128]{1,0:T(8,128)}, u32[]{:S(2)}) copy-start(f32[728,128]{1,0:T(8,128)} %copy-done.7) | copy-start | bytes 1118212
  24.5 1.0 %copy-start.10 = (f32[728,128]{1,0:T(8,128)S(1)}, f32[728,128]{1,0:T(8,128)}, u32[]{:S(2)}) copy-start(f32[728,128]{1,0:T(8,128)} %copy-done.9) | copy-start | bytes 1118212
  25.5 4.1 %copy-start.2 = (f32[16,32,512]{2,1,0:T(8,128)S(1)}, f32[16,32,512]{2,1,0:T(8,128)}, u32[]{:S(2)}) copy-start(f32[16,32,512]{2,1,0:T(8,128)} %std_ref.1) | copy-start | bytes 3145732
  28.7 0.7 %copy-start.11 = (f32[8,56,128]{2,1,0:T(8,128)}, f32[8,56,128]{2,1,0:T(8,128)S(1)}, u32[]{:S(2)}) copy-start(f32[8,56,128]{2,1,0:T(8,128)S(1)} %get-tuple-element.32.all_ref) | copy-start | bytes 688132
  29.6 0.8 %copy-start.14 = (s32[32,512]{1,0:T(8,128)S(1)}, s32[32,512]{1,0:T(8,128)}, u32[]{:S(2)}) copy-start(s32[32,512]{1,0:T(8,128)} %mask_ref.1) | copy-start | bytes 196612
  30.4 14.0 %copy-start = (f32[16,32,512]{2,1,0:T(8,128)S(1)}, f32[16,32,512]{2,1,0:T(8,128)}, u32[]{:S(2)}) copy-start(f32[16,32,512]{2,1,0:T(8,128)} %control_ref.1) | copy-start | bytes 3145732
  30.4 14.0 %copy-start.15 = (f32[16,16]{1,0:T(8,128)S(1)}, f32[16,16]{1,0:T(8,128)}, u32[]{:S(2)}) copy-start(f32[16,16]{1,0:T(8,128)} %v_ref.1) | copy-start | bytes 3076
  31.9 12.5 %copy-start.12 = (f32[8,56,128]{2,1,0:T(8,128)S(1)}, f32[8,56,128]{2,1,0:T(8,128)}, u32[]{:S(2)}) copy-start(f32[8,56,128]{2,1,0:T(8,128)} %copy-done.11) | copy-start | bytes 688132
  33.6 10.2 %collective-permute-start.3 = (f32[136,128]{1,0:T(8,128)S(1)}, f32[136,128]{1,0:T(8,128)S(1)}, u32[]{:S(2)}, u32[]{:S(2)}) collective-permute-start(f32[136,128]{1,0:T(8,128)S(1)} %get-tuple-element.31.own_ref), channel_id=1, source_target_pairs={{1,0},{2,1},{3,2},{4,3},{5,4},{6,5},{7,6},{8,7},{9,8},{10,9},{11,1... | collective-permute-start | bytes 208904 | tf_op jit(solution)/shard_map/ppermute | solution.py:562
  37.9 6.4 %collective-permute-start.2 = (f32[136,128]{1,0:T(8,128)S(1)}, f32[136,128]{1,0:T(8,128)S(1)}, u32[]{:S(2)}, u32[]{:S(2)}) collective-permute-start(f32[136,128]{1,0:T(8,128)S(1)} %get-tuple-element.31.own_ref), channel_id=1, source_target_pairs={{0,1},{1,2},{2,3},{3,4},{4,5},{5,6},{6,7},{7,8},{8,9},{9,10},{10,1... | collective-permute-start | bytes 208904 | tf_op jit(solution)/shard_map/ppermute | solution.py:561
  37.9 14.8 %all-to-all-start.1 = ((f32[16,1,128]{2,1,0:T(1,128)}), f32[16,1,128]{2,1,0:T(1,128)S(1)}, u32[]{:S(2)}, u32[]{:S(2)}) async-start(f32[16,1,128]{2,1,0:T(1,128)} %bitcast.8), calls=%async_computation.1 | async-start | bytes 16384 | tf_op jit(solution)/shard_map/all_to_all | solution.py:563
where the time goes:
time: 53.9 us; the launch traced here: 53.4 us
  Pallas kernels  21.9 us (41%)
  starting transfers between devices  19.4 us (36%)
  local copies, waits for them, and re-layouts  10.6 us (20%)
  between operations  0.83 us (2%)
  waiting for transfers between devices  0.6 us (1%)
    unnamed x40, local copies, waits for them, and re-layouts  9.83 us
    pallas_call x1, Pallas kernels, local(): call(second_kernel, shape(levels, cols, lat), [VMEM_SPEC] * 6, [field, fi...  8.32 us
    all_to_all x1, starting transfers between devices, local(): lax.all_to_all(departure[:, None, :], 'lon', split_axis=0, concat_axis=0,...  5.82 us
    ppermute x1, starting transfers between devices, local(): from_right = lax.ppermute(edge_left, 'lon', to_left)  5.06 us
    ppermute x1, starting transfers between devices, local(): spread_right = lax.ppermute(spread, 'lon', to_left)  4.38 us
    pallas_call x1, Pallas kernels, local(): call(head_kernel, (shape(parts, cols * levels, STEN), shape(3 * parts, co...  4.1 us
    all_to_all x1, starting transfers between devices, local(): recv = lax.all_to_all(sent, 'lon', split_axis=0, concat_axis=0, tiled=True)  3.62 us
    pallas_call x1, Pallas kernels, local(): call(inner_kernel, (shape(parts, (cols - 2 * halo) * levels, STEN), shape...  3.17 us
  transfers between devices with their start and end apart: 6, of which 1 were waited for; matrix products, arithmetic and copies ran while one was open for 0% of the time, Pallas kernels for 27%

commit v1 on v0

--- a/solution.py
+++ b/solution.py
@@ -270,14 +270,16 @@
 
 
 def inner_kernel(
-    mixed_ref, faces_ref, index_ref, value_ref, rinv_ref, count_ref, weights_ref,
+    ready, faces_ref, mixed_ref, index_ref, value_ref, rinv_ref, count_ref, weights_ref,
     inner_ref, strips_ref, sent_ref, a_ref, b_ref, lon_ref, lat_ref,
 ):
     parts, own_rows, _ = mixed_ref.shape
     cols = faces_ref.shape[1]
     levels = own_rows // cols
+    ready(1)
+    hold_faces(faces_ref, lon_ref, lat_ref, cols)
+    ready()
     pack(index_ref, value_ref, rinv_ref, count_ref, weights_ref, sent_ref)
-    hold_faces(faces_ref, lon_ref, lat_ref, cols)
     fill(a_ref, 0, [mixed_ref[q] for q in range(parts)])
 
     def save(turn, src):
@@ -301,12 +303,26 @@
     )
 
 
-def weights_kernel(place_ref, recv_ref, std_ref, mask_ref, out_ref, held_ref, pick_ref, std_rows, wet_rows):
+def to_row(column):
+    eye = iota((STEN, STEN), 0) == iota((STEN, STEN), 1)
+    return jnp.sum(jnp.where(eye, column, F32(0.0)), axis=0, keepdims=True)
+
+
+def to_column(row):
+    eye = iota((STEN, STEN), 0) == iota((STEN, STEN), 1)
+    return jnp.sum(jnp.where(eye, row, F32(0.0)), axis=1, keepdims=True)
+
+
+def departure_kernel(
+    ready, place_ref, mask_ref, std_ref, recv_ref, rows_ref,
+    spread_ref, departure_ref, ws_ref, held_ref, pick_ref, line_ref, std_rows, wet_rows,
+):
     owners, rows, _ = recv_ref.shape
     slots = rows // 2
     total = owners * slots
     levels, cols, lat = std_ref.shape
     parts = lat // STEN
+    ready(2)
     for s in range(parts):
         part = slice(s * STEN, (s + 1) * STEN)
         wet_rows[s * cols : (s + 1) * cols, :] = mask_ref[:, part].astype(F32)
@@ -323,9 +339,10 @@
             pick_ref[pl.ds(slot, 1), :] = value * wet
         return carry
 
+    ready()
     lax.fori_loop(0, owners, pick, 0)
     ws = recv_ref[:, 0:slots, :].reshape(total, STEN) * pick_ref[...]
-    out_ref[...] = ws
+    ws_ref[...] = ws
     place = spread_block(lat)
     segs = unpack_meta(recv_ref, slots, 2).astype(jnp.int32) & (parts - 1)
     for j in range(total // STEN):
@@ -336,19 +353,31 @@
         for q in range(parts):
             held_ref[q, part, :] = held[:, q * STEN : (q + 1) * STEN]
 
-
-def to_row(column):
-    eye = iota((STEN, STEN), 0) == iota((STEN, STEN), 1)
-    return jnp.sum(jnp.where(eye, column, F32(0.0)), axis=0, keepdims=True)
-
-
-def to_column(row):
-    eye = iota((STEN, STEN), 0) == iota((STEN, STEN), 1)
-    return jnp.sum(jnp.where(eye, row, F32(0.0)), axis=1, keepdims=True)
+    def pick_line(o, carry):
+        for k in range(slots):
+            slot = o * slots + k
+            row = place_ref[1, slot]
+            for q in range(parts):
+                line_ref[q, pl.ds(slot, 1), :] = rows_ref[q, pl.ds(row, 1), :]
+        return carry
+
+    lax.fori_loop(0, owners, pick_line, 0)
+    value, rinv, index, valid = (unpack_meta(recv_ref, slots, field) for field in range(4))
+    evolved = sum(line_ref[q] * held_ref[q] for q in range(parts))
+    evolved = jnp.sum(evolved, axis=1, keepdims=True)
+    departure = jnp.where(valid > 0.5, evolved - value, F32(0.0))
+    scaled = rinv * departure
+    spread_ref[0:total, :] = scaled * ws_ref[...]
+    spread_ref[total:, :] = jnp.zeros((spread_ref.shape[0] - total, STEN), F32)
+    for j in range(total // STEN):
+        part = slice(j * STEN, (j + 1) * STEN)
+        spread_ref[total + j : total + j + 1, :] = to_row(index[part])
+    lanes = jnp.where(iota((total, STEN), 1) == (iota((total, STEN), 0) & (slots - 1)), departure, F32(0.0))
+    departure_ref[...] = jnp.sum(lanes.reshape(owners, slots, STEN), axis=1)
 
 
 def edge_kernel(
-    inner_ref, strips_ref, from_left, from_right, faces_ref,
+    ready, faces_ref, from_left, from_right, strips_ref, inner_ref,
     rows_ref, all_ref, left_a, left_b, right_a, right_b, lon_ref, lat_ref,
 ):
     halo = PASSES
@@ -356,10 +385,13 @@
     parts = inner_ref.shape[0]
     cols = faces_ref.shape[1]
     edge = halo * levels
+    ready(3)
     join_faces(faces_ref, from_left, from_right, all_ref, levels)
     hold_faces(all_ref, lon_ref, lat_ref, cols + 2 * halo)
     fill(left_a, 0, [from_left[q * edge : (q + 1) * edge, :] for q in range(parts)])
     fill(right_a, 2 * levels, [from_right[q * edge : (q + 1) * edge, :] for q in range(parts)])
+
+    ready()
 
     def pair(turn, carry):
         for k, (left, left_to, right, right_to) in enumerate(
@@ -379,35 +411,6 @@
         rows_ref[q, 0:edge, :] = left_a[q, 0:edge, :]
         rows_ref[q, edge : cols * levels - edge, :] = inner_ref[q]
         rows_ref[q, cols * levels - edge :, :] = right_a[q, 2 * levels : 2 * levels + edge, :]
-
-
-def departure_kernel(place_ref, rows_ref, recv_ref, ws_ref, held_ref, spread_ref, departure_ref, pick_ref):
-    parts = rows_ref.shape[0]
-    owners, rows, _ = recv_ref.shape
-    slots = rows // 2
-    total = owners * slots
-
-    def pick(o, carry):
-        for k in range(slots):
-            slot = o * slots + k
-            row = place_ref[1, slot]
-            for q in range(parts):
-                pick_ref[q, pl.ds(slot, 1), :] = rows_ref[q, pl.ds(row, 1), :]
-        return carry
-
-    lax.fori_loop(0, owners, pick, 0)
-    value, rinv, index, valid = (unpack_meta(recv_ref, slots, field) for field in range(4))
-    evolved = sum(pick_ref[q] * held_ref[q] for q in range(parts))
-    evolved = jnp.sum(evolved, axis=1, keepdims=True)
-    departure = jnp.where(valid > 0.5, evolved - value, F32(0.0))
-    scaled = rinv * departure
-    spread_ref[0:total, :] = scaled * ws_ref[...]
-    spread_ref[total:, :] = jnp.zeros((spread_ref.shape[0] - total, STEN), F32)
-    for j in range(total // STEN):
-        part = slice(j * STEN, (j + 1) * STEN)
-        spread_ref[total + j : total + j + 1, :] = to_row(index[part])
-    lanes = jnp.where(iota((total, STEN), 1) == (iota((total, STEN), 0) & (slots - 1)), departure, F32(0.0))
-    departure_ref[...] = jnp.sum(lanes.reshape(owners, slots, STEN), axis=1)
 
 
 def second_kernel(
@@ -466,6 +469,40 @@
         cost_estimate=pl.CostEstimate(flops=flops, bytes_accessed=moved, transcendentals=0),
         compiler_params=pltpu.CompilerParams(vmem_limit_bytes=limit),
     )
+
+
+def call_loading(kernel, out_shape, smem, arrays, scratch, flops, moved):
+    count = len(arrays)
+    copies_of = [pltpu.VMEM(array.shape, array.dtype) for array in arrays]
+    outs = len(jax.tree.leaves(out_shape))
+
+    def body(*refs):
+        smem_refs, refs = refs[: len(smem)], refs[len(smem) :]
+        sources, refs = refs[:count], refs[count:]
+        out_refs, refs = refs[:outs], refs[outs:]
+        targets, sems, rest = refs[:count], refs[count], refs[count + 1 :]
+        copies = [pltpu.make_async_copy(a, b, sems.at[k]) for k, (a, b) in enumerate(zip(sources, targets))]
+        for copy in copies:
+            copy.start()
+        waited = [0]
+
+        def ready(n=count):
+            for copy in copies[waited[0] : n]:
+                copy.wait()
+            waited[0] = max(n, waited[0])
+
+        kernel(ready, *smem_refs, *targets, *out_refs, *rest)
+        ready()
+
+    return call(
+        body,
+        out_shape,
+        [SMEM_SPEC] * len(smem) + [pl.BlockSpec(memory_space=pltpu.HBM)] * count,
+        [*copies_of, pltpu.SemaphoreType.DMA((count,)), *scratch],
+        flops,
+        moved,
+        WHOLE_VMEM,
+    )(*smem, *arrays)
 
 
 def shape(*dims):
@@ -509,54 +546,48 @@
 
     inside = pltpu.VMEM((parts + 2, cols * levels, STEN), F32)
     wedge = pltpu.VMEM((parts + 2, (halo + 2) * levels, STEN), F32)
-    inner, strips, sent = call(
+    inner, strips, sent = call_loading(
         inner_kernel,
         (
             shape(parts, (cols - 2 * halo) * levels, STEN), shape(PASSES, 2, 2 * parts, levels, STEN),
             shape(owners, 2 * slots, STEN),
         ),
-        [VMEM_SPEC] * 7,
+        [],
+        [faces, mixed, block_index[0].T, obs_value[0].T, obs_rinv[0].T, obs_count, weights[0]],
         [
             inside, inside,
             pltpu.VMEM((parts, cols * 8, STEN), F32), pltpu.VMEM((parts + 1, cols * 8, STEN), F32),
         ],
         5 * PASSES * cells, PASSES * 4 * cells,
-    )(
-        mixed, faces, block_index[0].T, obs_value[0].T, obs_rinv[0].T, obs_count, weights[0]
     )
     recv = lax.all_to_all(sent, "lon", split_axis=0, concat_axis=0, tiled=True)
     field = pltpu.VMEM((parts + 2, width * levels, STEN), F32)
     faces_held = [pltpu.VMEM((parts, width * 8, STEN), F32), pltpu.VMEM((parts + 1, width * 8, STEN), F32)]
-    rows, all_faces = call(
+    rows, all_faces = call_loading(
         edge_kernel,
         (shape(parts, cols * levels, STEN), shape(2 * parts, -(-width // 8) * 8, STEN)),
-        [VMEM_SPEC] * 5,
+        [],
+        [faces, from_left, from_right, strips, inner],
         [wedge, wedge, wedge, wedge, *faces_held],
         5 * PASSES * cells, PASSES * 4 * cells,
-    )(inner, strips, from_left, from_right, faces)
+    )
     recv, rows = lax.optimization_barrier((recv, rows))
     index = recv[:, slots, 2 * slots : 3 * slots].reshape(total).astype(jnp.int32)
     level, column, _ = block_place(index, cols, parts)
     places = jnp.stack([index, column * levels + level])
-    ws, held = call(
-        weights_kernel,
-        (shape(total, STEN), shape(parts, total, STEN)),
-        [SMEM_SPEC] + [VMEM_SPEC] * 3,
+    extra = -(-total // (8 * STEN)) * 8
+    spread, departure = call_loading(
+        departure_kernel,
+        (shape(total + extra, STEN), shape(owners, STEN)),
+        [places],
+        [sea_mask, std_field, recv, rows],
         [
-            pltpu.VMEM((total, STEN), F32), pltpu.VMEM((levels * cols * parts, STEN), F32),
+            pltpu.VMEM((total, STEN), F32), pltpu.VMEM((parts, total, STEN), F32), pltpu.VMEM((total, STEN), F32),
+            pltpu.VMEM((parts, total, STEN), F32), pltpu.VMEM((levels * cols * parts, STEN), F32),
             pltpu.VMEM((cols * parts, STEN), F32),
         ],
-        6 * total * STEN * lat, 4 * 4 * cells,
-    )(places, recv, std_field, sea_mask)
-
-    extra = -(-total // (8 * STEN)) * 8
-    spread, departure = call(
-        departure_kernel,
-        (shape(total + extra, STEN), shape(owners, STEN)),
-        [SMEM_SPEC] + [VMEM_SPEC] * 4,
-        [pltpu.VMEM((parts, total, STEN), F32)],
         8 * total * lat, 4 * 4 * total * lat,
-    )(places, rows, recv, ws, held)
+    )
 
     spread_left = lax.ppermute(spread, "lon", to_right)
     spread_right = lax.ppermute(spread, "lon", to_left)

time: 53.9 us -> 52.5 us (0.974)
  local copies, waits for them, and re-layouts: 10.6 us -> 2.53 us
  Pallas kernels: 21.9 us -> 27.8 us
  waiting for transfers between devices: 0.6 us -> 2.14 us
  starting transfers between devices: 19.4 us -> 18.1 us
  other arithmetic: 0.11 us -> 0.68 us
    unnamed x40 -> x14, local copies, waits for them, and re-layouts: 9.83 us -> 1.75 us
    pallas_call x4 -> x3, Pallas kernels: 9.44 us -> 15.4 us  [call_loading(): call(body, out_shape, [SMEM_SPEC] * len(smem) + [pl.BlockSpec(memory_spac...]
    all_to_all x1, waiting for transfers between devices: 0.01 us -> 1.33 us  [local(): recv = lax.all_to_all(sent, 'lon', split_axis=0, concat_axis=0, tiled=True)]
    ppermute x1, starting transfers between devices: 4.38 us -> 3.12 us  [local(): spread_right = lax.ppermute(spread, 'lon', to_left)]
    another operation x1, other arithmetic: 0.01 us -> 0.57 us  [local(): places = jnp.stack([index, column * levels + level])]
  transfers between devices with their start and end apart: 6 -> 6, of which waited for: 1 -> 2; matrix products, arithmetic and copies ran while one was open for 0% -> 0% of each run, Pallas kernels for 27% -> 37%
where the time goes in v1:
time: 52.5 us; the launch traced here: 52 us
  Pallas kernels  27.8 us (53%)
  starting transfers between devices  18.1 us (34%)
  local copies, waits for them, and re-layouts  2.53 us (5%)
  waiting for transfers between devices  2.14 us (4%)
  between operations  0.77 us (1%)
  other arithmetic  0.68 us (1%)
    pallas_call x3, Pallas kernels, call_loading(): call(body, out_shape, [SMEM_SPEC] * len(smem) + [pl.BlockSpec(memory_spac...  15.4 us
    pallas_call x1, Pallas kernels, local(): call(second_kernel, shape(levels, cols, lat), [VMEM_SPEC] * 6, [field, fi...  8.31 us
    all_to_all x1, starting transfers between devices, local(): lax.all_to_all(departure[:, None, :], 'lon', split_axis=0, concat_axis=0,...  5.82 us
    ppermute x1, starting transfers between devices, local(): from_right = lax.ppermute(edge_left, 'lon', to_left)  5.06 us
    pallas_call x1, Pallas kernels, local(): call(head_kernel, (shape(parts, cols * levels, STEN), shape(3 * parts, co...  4.04 us
    all_to_all x1, starting transfers between devices, local(): recv = lax.all_to_all(sent, 'lon', split_axis=0, concat_axis=0, tiled=True)  3.63 us
    ppermute x1, starting transfers between devices, local(): spread_right = lax.ppermute(spread, 'lon', to_left)  3.12 us
    unnamed x14, local copies, waits for them, and re-layouts  1.75 us
  transfers between devices with their start and end apart: 6, of which 2 were waited for; matrix products, arithmetic and copies ran while one was open for 0% of the time, Pallas kernels for 37%

profile of v1, /device:TPU:0, one launch (start us, length us, event | category | flops | bytes accessed | tf_op | source)
XLA Modules:
  0.0 52.0 jit_solution(11107874121054294720)
XLA Ops:
  0.6 4.0 %shard_map.122 = (f32[4,512,128]{2,1,0:T(8,128)}, f32[12,32,128]{2,1,0:T(8,128)}, f32[728,128]{1,0:T(8,128)}, f32[728,128]{1,0:T(8,128)}) custom-call(s32[32,512]{1,0:T(8,128)} %refs_1_.1, f32[32,512]{1,0:T(8,128)} %klon_hbm.1, f32[32,512]{1,0:T(8,128)} %klat_hbm.1, f32[16,16]{1,0:T(8,128)} %v_ref.1, f32[16,32,512]{2,1,0:T(8,128)} %control_ref.1), custom_call_target="tpu_custom_call" | custom-call | flops 2617245696 | bytes 13631488 | tf_op jit(solution)/shard_map/pallas_call | solution.py:531
  4.7 0.5 collective-permute-start
  5.2 5.1 %collective-permute-start.1 = (f32[728,128]{1,0:T(8,128)}, f32[728,128]{1,0:T(8,128)S(1)}, u32[]{:S(2)}, u32[]{:S(2)}) collective-permute-start(f32[728,128]{1,0:T(8,128)} %get-tuple-element.21), channel_id=1, source_target_pairs={{1,0},{2,1},{3,2},{4,3},{5,4},{6,5},{7,6},{8,7},{9,8},{10,9},{11,1... | collective-permute-start | bytes 1118216 | tf_op jit(solution)/shard_map/ppermute | solution.py:545
  10.2 5.5 %shard_map.123 = (f32[4,192,128]{2,1,0:T(8,128)}, f32[10,2,8,16,128]{4,3,2,1,0:T(8,128)}, f32[16,16,128]{2,1,0:T(8,128)}) custom-call(f32[12,32,128]{2,1,0:T(8,128)} %get-tuple-element.17.refs_0_, f32[4,512,128]{2,1,0:T(8,128)} %get-tuple-element.18.refs_1_, s32[8,16]{1,0:T(8,128)} %bitcast.17, f32[8,16]{1,0:T(8,128)} %bitcast.18, f32[8,16]{1,0:T(8,128)} %bitcast.19, ...), custom_call_target="tpu_custom_call" | custom-call | flops 21299200 | bytes 17039360 | tf_op jit(solution)/shard_map/pallas_call | solution.py:497
  15.7 3.6 %all-to-all-start = ((f32[16,16,128]{2,1,0:T(8,128)}), f32[16,16,128]{2,1,0:T(8,128)S(1)}, u32[]{:S(2)}, u32[]{:S(2)}) async-start(f32[16,16,128]{2,1,0:T(8,128)} %get-tuple-element.19), calls=%async_computation | async-start | bytes 262144 | tf_op jit(solution)/shard_map/all_to_all | solution.py:563
  19.3 0.0 collective-permute-done.refs_1_
  19.4 0.0 copy-start.5
  19.4 0.0 collective-permute-done.1.refs_2_
  19.4 0.0 copy-start.6
  19.4 0.7 %copy-done.5 = f32[728,128]{1,0:T(8,128)} copy-done((f32[728,128]{1,0:T(8,128)}, f32[728,128]{1,0:T(8,128)S(1)}, u32[]{:S(2)}) %copy-start.5) | copy-done | bytes 372760
  20.1 0.1 copy-done.6
  20.2 5.7 %shard_map.124 = (f32[4,512,128]{2,1,0:T(8,128)}, f32[8,56,128]{2,1,0:T(8,128)}) custom-call(f32[12,32,128]{2,1,0:T(8,128)} %get-tuple-element.17.refs_0_, f32[728,128]{1,0:T(8,128)} %copy-done.5, f32[728,128]{1,0:T(8,128)} %copy-done.6, f32[10,2,8,16,128]{4,3,2,1,0:T(8,128)} %get-tuple-element.22.refs_3_, f32[4,192,128]{2,1,0:T(8,128)} %get-tuple-element.23.refs_4_), custom_call_target="tpu_custom_call" | custom-call | flops 21299200 | bytes 17039360 | tf_op jit(solution)/shard_map/pallas_call | solution.py:497
  25.9 0.0 copy-start
  25.9 0.0 copy-start.1
  25.9 0.0 copy-start.3
  26.0 1.3 %all-to-all-done.refs_3_ = f32[16,16,128]{2,1,0:T(8,128)S(1)} async-done(((f32[16,16,128]{2,1,0:T(8,128)}), f32[16,16,128]{2,1,0:T(8,128)S(1)}, u32[]{:S(2)}, u32[]{:S(2)}) %all-to-all-start) | async-done | bytes 131104 | tf_op jit(solution)/shard_map/all_to_all | solution.py:563
  27.3 0.1 convert_reduce_fusion
  27.4 0.1 convert_element_type.18
  27.5 0.6 %pad_add_fusion.refs_0_ = s32[2,128]{1,0:T(2,128)} fusion(s32[1,128]{1,0:T(1,128)S(1)} %shift-right-logical_add_fusion, s32[1,128]{1,0:T(1,128)S(1)} %convert_element_type.18), kind=kLoop, calls=%fused_computation.2 | loop fusion | flops 256 | bytes 2048 | tf_op jit(solution)/shard_map/stack | solution.py:577
  28.1 0.0 copy-done.4
  28.1 4.3 %shard_map.125 = (f32[136,128]{1,0:T(8,128)}, f32[16,128]{1,0:T(8,128)}) custom-call(s32[2,128]{1,0:T(2,128)} %pad_add_fusion.refs_0_, s32[32,512]{1,0:T(8,128)} %refs_1_.1, f32[16,32,512]{2,1,0:T(8,128)} %refs_2_.1, f32[16,16,128]{2,1,0:T(8,128)} %copy-done.4, f32[4,512,128]{2,1,0:T(8,128)} %get-tuple-element.26.refs_4_), custom_call_target="tpu_custom_call" | custom-call | flops 524288 | bytes 1048576 | tf_op jit(solution)/shard_map/pallas_call | solution.py:497
  32.4 3.1 %collective-permute-start.3 = (f32[136,128]{1,0:T(8,128)}, f32[136,128]{1,0:T(8,128)S(1)}, u32[]{:S(2)}, u32[]{:S(2)}) collective-permute-start(f32[136,128]{1,0:T(8,128)} %get-tuple-element.27.own_ref), channel_id=1, source_target_pairs={{1,0},{2,1},{3,2},{4,3},{5,4},{6,5},{7,6},{8,7},{9,8},{10,9},{11,1... | collective-permute-start | bytes 208904 | tf_op jit(solution)/shard_map/ppermute | solution.py:593
  35.5 0.0 collective-permute-start.2
  35.5 5.8 %all-to-all-start.1 = ((f32[16,1,128]{2,1,0:T(1,128)}), f32[16,1,128]{2,1,0:T(1,128)S(1)}, u32[]{:S(2)}, u32[]{:S(2)}) async-start(f32[16,1,128]{2,1,0:T(1,128)} %bitcast.16), calls=%async_computation.1 | async-start | bytes 16384 | tf_op jit(solution)/shard_map/all_to_all | solution.py:594
  41.3 0.0 collective-permute-done.3.right_ref
  41.3 0.8 %collective-permute-done.2.left_ref = f32[136,128]{1,0:T(8,128)S(1)} collective-permute-done((f32[136,128]{1,0:T(8,128)}, f32[136,128]{1,0:T(8,128)S(1)}, u32[]{:S(2)}, u32[]{:S(2)}) %collective-permute-start.2) | collective-permute-done | bytes 69664 | tf_op jit(solution)/shard_map/ppermute | solution.py:592
  42.1 0.0 copy-done.1
  42.2 0.9 %copy-done.2 = f32[136,128]{1,0:T(8,128)S(1)} copy-done((f32[136,128]{1,0:T(8,128)S(1)}, f32[136,128]{1,0:T(8,128)}, u32[]{:S(2)}) %copy-start.2) | copy-done | bytes 69656
  43.0 8.3 %shard_map.126 = f32[16,32,512]{2,1,0:T(8,128)} custom-call(f32[16,16]{1,0:T(8,128)S(1)} %copy-done.3, f32[16,32,512]{2,1,0:T(8,128)S(1)} %copy-done, f32[136,128]{1,0:T(8,128)S(1)} %copy-done.2, f32[136,128]{1,0:T(8,128)S(1)} %collective-permute-done.2.left_ref, f32[136,128]{1,0:T(8,128)S(1)} %collective-permute-done.3.right_ref, f32[8,56,128]{2,1,0:T(8,128)S(1)} %copy-done.1), custom_call_target="tpu_custom_call" | custom-call | flops 42598400 | bytes 34078720 | tf_op jit(solution)/shard_map/pallas_call | solution.py:596
  51.3 0.0 all-to-all-done.1
  51.4 0.1 copy.16
  51.5 0.6 %slice_bitcast_fusion = f32[1,16,8]{1,2,0:T(8,128)} fusion(f32[16,1,128]{0,2,1:T(8,128)S(1)} %copy.16), kind=kLoop, calls=%fused_computation.1 | loop fusion | bytes 1024 | tf_op jit(solution)/shard_map/broadcast_in_dim;squeeze | solution.py:601
  (5 shorter events, 0.0 us)
Async XLA Ops:
  4.7 14.7 %collective-permute-start = (f32[728,128]{1,0:T(8,128)}, f32[728,128]{1,0:T(8,128)S(1)}, u32[]{:S(2)}, u32[]{:S(2)}) collective-permute-start(f32[728,128]{1,0:T(8,128)} %get-tuple-element.20), channel_id=1, source_target_pairs={{0,1},{1,2},{2,3},{3,4},{4,5},{5,6},{6,7},{7,8},{8,9},{9,10},{10,1... | collective-permute-start | bytes 1118216 | tf_op jit(solution)/shard_map/ppermute | solution.py:544
  5.2 14.2 %collective-permute-start.1 = (f32[728,128]{1,0:T(8,128)}, f32[728,128]{1,0:T(8,128)S(1)}, u32[]{:S(2)}, u32[]{:S(2)}) collective-permute-start(f32[728,128]{1,0:T(8,128)} %get-tuple-element.21), channel_id=1, source_target_pairs={{1,0},{2,1},{3,2},{4,3},{5,4},{6,5},{7,6},{8,7},{9,8},{10,9},{11,1... | collective-permute-start | bytes 1118216 | tf_op jit(solution)/shard_map/ppermute | solution.py:545
  15.7 11.6 %all-to-all-start = ((f32[16,16,128]{2,1,0:T(8,128)}), f32[16,16,128]{2,1,0:T(8,128)S(1)}, u32[]{:S(2)}, u32[]{:S(2)}) async-start(f32[16,16,128]{2,1,0:T(8,128)} %get-tuple-element.19), calls=%async_computation | async-start | bytes 262144 | tf_op jit(solution)/shard_map/all_to_all | solution.py:563
  19.4 0.7 %copy-start.5 = (f32[728,128]{1,0:T(8,128)}, f32[728,128]{1,0:T(8,128)S(1)}, u32[]{:S(2)}) copy-start(f32[728,128]{1,0:T(8,128)S(1)} %collective-permute-done.refs_1_) | copy-start | bytes 1118212
  19.4 0.9 %copy-start.6 = (f32[728,128]{1,0:T(8,128)}, f32[728,128]{1,0:T(8,128)S(1)}, u32[]{:S(2)}) copy-start(f32[728,128]{1,0:T(8,128)S(1)} %collective-permute-done.1.refs_2_) | copy-start | bytes 1118212
  25.9 16.2 %copy-start = (f32[16,32,512]{2,1,0:T(8,128)S(1)}, f32[16,32,512]{2,1,0:T(8,128)}, u32[]{:S(2)}) copy-start(f32[16,32,512]{2,1,0:T(8,128)} %control_ref.1) | copy-start | bytes 3145732
  25.9 16.2 %copy-start.1 = (f32[8,56,128]{2,1,0:T(8,128)S(1)}, f32[8,56,128]{2,1,0:T(8,128)}, u32[]{:S(2)}) copy-start(f32[8,56,128]{2,1,0:T(8,128)} %get-tuple-element.28.all_ref) | copy-start | bytes 688132
  25.9 16.2 %copy-start.3 = (f32[16,16]{1,0:T(8,128)S(1)}, f32[16,16]{1,0:T(8,128)}, u32[]{:S(2)}) copy-start(f32[16,16]{1,0:T(8,128)} %v_ref.1) | copy-start | bytes 3076
  27.3 0.8 %copy-start.4 = (f32[16,16,128]{2,1,0:T(8,128)}, f32[16,16,128]{2,1,0:T(8,128)S(1)}, u32[]{:S(2)}) copy-start(f32[16,16,128]{2,1,0:T(8,128)S(1)} %all-to-all-done.refs_3_) | copy-start | bytes 393220
  32.4 9.0 %collective-permute-start.3 = (f32[136,128]{1,0:T(8,128)}, f32[136,128]{1,0:T(8,128)S(1)}, u32[]{:S(2)}, u32[]{:S(2)}) collective-permute-start(f32[136,128]{1,0:T(8,128)} %get-tuple-element.27.own_ref), channel_id=1, source_target_pairs={{1,0},{2,1},{3,2},{4,3},{5,4},{6,5},{7,6},{8,7},{9,8},{10,9},{11,1... | collective-permute-start | bytes 208904 | tf_op jit(solution)/shard_map/ppermute | solution.py:593
  35.5 6.6 %collective-permute-start.2 = (f32[136,128]{1,0:T(8,128)}, f32[136,128]{1,0:T(8,128)S(1)}, u32[]{:S(2)}, u32[]{:S(2)}) collective-permute-start(f32[136,128]{1,0:T(8,128)} %get-tuple-element.27.own_ref), channel_id=1, source_target_pairs={{0,1},{1,2},{2,3},{3,4},{4,5},{5,6},{6,7},{7,8},{8,9},{9,10},{10,1... | collective-permute-start | bytes 208904 | tf_op jit(solution)/shard_map/ppermute | solution.py:592
  35.5 15.8 %all-to-all-start.1 = ((f32[16,1,128]{2,1,0:T(1,128)}), f32[16,1,128]{2,1,0:T(1,128)S(1)}, u32[]{:S(2)}, u32[]{:S(2)}) async-start(f32[16,1,128]{2,1,0:T(1,128)} %bitcast.16), calls=%async_computation.1 | async-start | bytes 16384 | tf_op jit(solution)/shard_map/all_to_all | solution.py:594
  42.2 0.9 %copy-start.2 = (f32[136,128]{1,0:T(8,128)S(1)}, f32[136,128]{1,0:T(8,128)}, u32[]{:S(2)}) copy-start(f32[136,128]{1,0:T(8,128)} %get-tuple-element.27.own_ref) | copy-start | bytes 208900
